TPU v7x, 512 devices: a whole 4x8x8 slice. The times are simulated.
512 devices in a mesh: tm: 64 (over z, y), head: 8 (over x, core).
Axes of the slice: x: 4, y: 8, z: 8, core: 2. Of those that a mesh axis runs over, the one named last changes fastest.
Arguments:
- queries: bfloat16 [10240, 3072], P('tm', 'head'), may hold values from -200 to 200
- keys: bfloat16 [10240, 3072], P('tm', 'head'), may hold values from -8 to 8
- values: bfloat16 [10240, 3072], P('tm', 'head'), may hold values from -6 to 6
- block_group: int32 [64], replicated, may hold values from 0 to 3, as said below
- group_mask: int32 [4, 4], replicated, may hold values from 0 to 1, as said below
- teacher_gain: float32 [3072], P('head'), may hold values from 0.25 to 1.75
Outputs:
- student_out: bfloat16 [10240, 3072], P('tm', 'head')
- teacher_out: bfloat16 [10240, 3072], P('tm', 'head')
- gap: float32 [10240], P('tm')
Inputs may be any that keep to these rules, and one draw needn't show every extreme that they name: `block_group`: never falls from one block to the next, starts at 0 and ends at 3; every group holds one block or more. `group_mask`: entry (i, j) is 1 where j == i or j == i - 1, 0 where j > i; the other entries are 0 or 1.
All inputs are finite; a program needn't handle non-finite values.
Results may differ from a plain program's by a relative error of at most 0.0095.
Values may be sent and summed in bfloat16 or wider, within the bound.
A program may use at most 128 MiB of HBM per device.

v0:
```python
import jax
import jax.numpy as jnp
from jax import lax
from jax.sharding import PartitionSpec as P

HD = 128


def update_state(state, query_heads, key_heads, value_heads, permitted):
    largest, denom, accumul = state
    scores = jnp.einsum(
        "qhd,khd->hqk", query_heads, key_heads, preferred_element_type=jnp.float32
    ) * HD ** (-0.5)
    scores = jnp.where(permitted, scores, jnp.float32(-1e30))
    new_largest = jnp.maximum(largest, jnp.max(scores, axis=-1))
    weights = jnp.where(permitted, jnp.exp(scores - new_largest[..., None]), jnp.float32(0.0))
    rescale = jnp.exp(largest - new_largest)
    denom = denom * rescale + jnp.sum(weights, axis=-1)
    accumul = accumul * rescale[..., None] + jnp.einsum(
        "hqk,khd->hqd",
        weights.astype(jnp.bfloat16),
        value_heads,
        preferred_element_type=jnp.float32,
    )
    return (new_largest, denom, accumul)


def finish(state, row_count, breadth):
    largest, denom, accumul = state
    mixed = (accumul / denom[..., None]).astype(jnp.bfloat16)
    return mixed.transpose(1, 0, 2).reshape(row_count, breadth)


def on_device(queries, keys, values, block_group, group_mask, teacher_gain):
    row_count, breadth = queries.shape
    head_count = breadth // HD
    block_count = block_group.shape[0]
    group_count = group_mask.shape[0]
    device_slot = lax.axis_index("tm")
    block_slots = jnp.arange(block_count, dtype=jnp.int32)
    group_slots = jnp.arange(group_count, dtype=jnp.int32)
    own_group = jnp.sum(jnp.where(block_slots == device_slot, block_group, 0))
    row_allow = jnp.sum(jnp.where(group_slots[:, None] == own_group, group_mask, 0), axis=0)
    block_allow = jnp.sum(
        jnp.where(block_group[:, None] == group_slots[None, :], row_allow[None, :], 0), axis=1
    )
    teacher_q = (queries.astype(jnp.float32) * teacher_gain[None, :]).astype(jnp.bfloat16)
    student_heads = queries.reshape(row_count, head_count, HD)
    teacher_heads = teacher_q.reshape(row_count, head_count, HD)
    start_state = (
        jnp.full((head_count, row_count), -1e30, jnp.float32),
        jnp.zeros((head_count, row_count), jnp.float32),
        jnp.zeros((head_count, row_count, HD), jnp.float32),
    )

    def absorb(states, key_piece, value_piece, offset):
        piece_rows = key_piece.shape[0]
        owner = (offset + jnp.arange(piece_rows, dtype=jnp.int32)) // row_count
        permitted = (
            jnp.sum(
                jnp.where(owner[:, None] == block_slots[None, :], block_allow[None, :], 0), axis=1
            )
            == 1
        )
        key_heads = key_piece.reshape(piece_rows, head_count, HD)
        value_heads = value_piece.reshape(piece_rows, head_count, HD)
        student_state = lax.cond(
            jnp.any(permitted),
            lambda state: update_state(
                state, student_heads, key_heads, value_heads, permitted[None, None, :]
            ),
            lambda state: state,
            states[0],
        )
        everywhere = jnp.ones((1, 1, piece_rows), dtype=bool)
        teacher_state = update_state(states[1], teacher_heads, key_heads, value_heads, everywhere)
        return (student_state, teacher_state)

    all_keys, all_values = (
        lax.all_gather(keys, "tm", axis=0, tiled=True),
        lax.all_gather(values, "tm", axis=0, tiled=True),
    )
    total_rows = all_keys.shape[0]
    block_rows = min(512, total_rows)
    block_total = total_rows // block_rows
    key_blocks = all_keys.reshape(block_total, block_rows, breadth)
    value_blocks = all_values.reshape(block_total, block_rows, breadth)

    def scan_block(states, operands):
        block_number, key_piece, value_piece = operands
        return (absorb(states, key_piece, value_piece, block_number * block_rows), None)

    states, unused = lax.scan(
        scan_block,
        (start_state, start_state),
        (jnp.arange(block_total, dtype=jnp.int32), key_blocks, value_blocks),
    )
    student_out = finish(states[0], row_count, breadth)
    teacher_out = finish(states[1], row_count, breadth)
    difference = teacher_out.astype(jnp.float32) - student_out.astype(jnp.float32)
    partial_sums = jnp.sum(difference * difference, axis=-1)
    gap = lax.psum(partial_sums, "head") / (breadth * lax.axis_size("head"))
    return (student_out, teacher_out, gap)


def solution(mesh):
    placed = (P("tm", "head"), P("tm", "head"), P("tm", "head"), P(), P(), P("head"))
    return jax.shard_map(
        on_device,
        mesh=mesh,
        in_specs=placed,
        out_specs=(P("tm", "head"), P("tm", "head"), P("tm")),
        check_vma=False,
    )
```

profile of v0, /device:TPU:32, one launch (start us, length us, event | category | flops | bytes accessed | tf_op | source)
XLA Modules:
  0.0 358.0 jit_solution(1472515661406311069)
XLA Ops:
  7.2 0.7 all-gather.3.cloned.1.call-update
  7.9 0.7 all-gather.5.cloned.1.call-update
  8.7 1.3 fusion.18
  10.0 0.6 iota_compare_fusion.2
  10.6 0.8 select_reduce_fusion.2
  11.4 0.7 select_reduce_fusion.1
  12.1 1.0 copy_bitcast_fusion.2
  13.2 99.0 %all-gather.3.cloned.1.call-done = bf16[10240,384]{1,0:T(8,128)(2,1)} async-done(((bf16[160,384]{1,0:T(8,128)(2,1)}), bf16[10240,384]{1,0:T(8,128)(2,1)}) %all-gather.3.cloned.1.call-update) | async-done | bytes 7864336 | tf_op jit(solution)/shard_map/all_gather | solution.py:80
  112.2 98.0 %all-gather.5.cloned.1.call-done = bf16[10240,384]{1,0:T(8,128)(2,1)} async-done(((bf16[160,384]{1,0:T(8,128)(2,1)}), bf16[10240,384]{1,0:T(8,128)(2,1)}) %all-gather.5.cloned.1.call-update) | async-done | bytes 7864336 | tf_op jit(solution)/shard_map/all_gather | solution.py:81
  210.2 124.0 %while.23 = (s32[]{:T(128)}, f32[3,160]{1,0:T(4,128)S(1)}, f32[3,160]{1,0:T(4,128)S(1)}, f32[3,160,128]{2,1,0:T(8,128)S(1)}, f32[3,160]{1,0:T(4,128)S(1)}, /*ind...) while((s32[]{:T(128)}, f32[3,160]{1,0:T(4,128)S(1)}, ...), condition=%wide.region_12.13_spmd.clone, body=%wide.region_3.12_spmd.clone.sunk | while | flops 255758624 | bytes 11917887 | solution.py:93
  211.5 0.6 fusion.46
  212.8 1.2 constant_dynamic-slice_fusion.3
  214.4 1.2 conditional.3
  218.2 0.6 fusion.46
  219.5 1.2 constant_dynamic-slice_fusion.3
  221.1 1.2 conditional.3
  224.9 0.6 fusion.46
  226.2 1.2 constant_dynamic-slice_fusion.3
  227.8 1.2 conditional.3
  232.9 1.2 constant_dynamic-slice_fusion.3
  234.5 1.2 conditional.3
  239.6 1.2 constant_dynamic-slice_fusion.3
  241.2 1.2 conditional.3
  246.2 1.2 constant_dynamic-slice_fusion.3
  247.8 1.2 conditional.3
  252.9 1.2 constant_dynamic-slice_fusion.3
  254.5 1.2 conditional.3
  259.6 1.2 constant_dynamic-slice_fusion.3
  261.2 1.2 conditional.3
  266.3 1.2 constant_dynamic-slice_fusion.3
  267.9 1.2 conditional.3
  273.0 1.2 constant_dynamic-slice_fusion.3
  274.6 1.2 conditional.3
  279.6 1.2 constant_dynamic-slice_fusion.3
  281.3 1.2 conditional.3
  286.3 1.2 constant_dynamic-slice_fusion.3
  287.9 1.2 conditional.3
  293.0 1.2 constant_dynamic-slice_fusion.3
  298.5 1.2 constant_dynamic-slice_fusion.3
  304.0 1.2 constant_dynamic-slice_fusion.3
  309.5 1.2 constant_dynamic-slice_fusion.3
  314.9 1.2 constant_dynamic-slice_fusion.3
  320.4 1.2 constant_dynamic-slice_fusion.3
  325.9 1.2 constant_dynamic-slice_fusion.3
  331.4 1.2 constant_dynamic-slice_fusion.3
  334.2 0.8 copy_bitcast_fusion
  335.3 0.8 copy_bitcast_fusion.1
  336.1 14.5 %psum.7 = f32[160]{0:T(256)S(1)} all-reduce(f32[160]{0:T(256)S(1)} %multiply_reduce_fusion), channel_id=1, replica_groups=mesh['tm'=64,'head'=8] {'head'}, use_global_device_ids=true, to_apply=%region_14.15 | all-reduce | flops 160 | bytes 1280 | tf_op jit(solution)/shard_map/psum | solution.py:102
  (328 shorter events, 71.1 us)
Async XLA Ops:
  7.2 105.0 %all-gather.3.cloned.1.call-start = ((), (), s32[]{:S(2)}) async-start(), calls=%async_computation | async-start | bytes 7987200 | tf_op jit(solution)/shard_map/all_gather | solution.py:80
  7.9 202.2 %all-gather.5.cloned.1.call-start = ((), (), s32[]{:S(2)}) async-start(), calls=%async_computation.1 | async-start | bytes 7987200 | tf_op jit(solution)/shard_map/all_gather | solution.py:81
Sparse Core Ops, SparseCore 0:
  11.0 101.1 all-gather.2
  115.2 94.9 all-gather.4
where the time goes:
time: 363 us; the launch traced here: 358 us
  waiting for transfers between devices  198 us (55%)
  local copies, waits for them, and re-layouts  43.7 us (12%)
  other arithmetic  35 us (10%)
  loops' own time  28.1 us (8%)
  matrix products  24.3 us (7%)
  blocking collectives  14.5 us (4%)
  between operations  14.1 us (4%)
    all_gather x1, waiting for transfers between devices, on_device(): lax.all_gather(keys, 'tm', axis=0, tiled=True)  99 us
    all_gather x1, waiting for transfers between devices, on_device(): lax.all_gather(values, 'tm', axis=0, tiled=True)  98 us
    dynamic_slice x80, local copies, waits for them, and re-layouts, on_device(): lax.scan(scan_block, (start_state, start_state), (jnp.arange(block_total,...  43.6 us
    another operation x1, loops' own time, on_device(): lax.scan(scan_block, (start_state, start_state), (jnp.arange(block_total,...  27.5 us
    psum x1, blocking collectives, on_device(): gap = lax.psum(partial_sums, 'head') / (breadth * lax.axis_size('head'))  14.5 us
    reduce_or x20, other arithmetic, absorb(): jnp.any(permitted)  12.7 us
    dot_general x32, matrix products, update_state(): jnp.einsum('qhd,khd->hqk', query_heads, key_heads, preferred_element_type...  12.5 us
    reduce_sum x32, other arithmetic, update_state(): denom = denom * rescale + jnp.sum(weights, axis=-1)  12.3 us
  transfers between devices with their start and end apart: 2, of which 2 were waited for; matrix products, arithmetic and copies ran while one was open for 1% of the time, Pallas kernels for 0%

commit v1 on v0

v1 whole, which is shorter than its diff:
```python
import functools
import math

import jax
import jax.numpy as jnp
from jax import lax
from jax.experimental import pallas as pl
from jax.experimental.pallas import tpu as pltpu
from jax.sharding import PartitionSpec as P

HD = 128
RING = 8
HEADS_DEV = 3
PEERS = 8
ROWS = 160
STAT = 16
KEYS = RING * ROWS
UNITS = RING * HEADS_DEV
SCALE = math.log2(math.e) / math.sqrt(HD)
EMPTY = -1e30
MESH = pl.DeviceIdType.MESH
NT = (((1,), (1,)), ((), ()))
TN = (((0,), (0,)), ((), ()))
BF = jnp.bfloat16
F32 = jnp.float32


def kernel(
    q_ref, k_ref, v_ref, group_ref, mask_ref, gain_ref,
    s_out, t_out, gap_out,
    k_all, v_all, q_all, bias, gains, score0, score1, part, lse, inbox, outbox, gap_sum, gap_in,
    g_send, g_recv, o_send, o_recv, d_send, d_recv,
):
    tm = lax.axis_index("tm")
    head = lax.axis_index("head")
    core = lax.rem(head, 2)
    zpos, ypos = lax.div(tm, RING), lax.rem(tm, RING)
    kpos = jnp.where(core == 0, zpos, ypos)
    qpos = jnp.where(core == 0, ypos, zpos)

    def device(kp, qp):
        return jnp.where(core == 0, kp * RING + qp, qp * RING + kp)

    def wrap(x):
        return lax.rem(x + 2 * RING, RING)

    k_near = {1: device(wrap(kpos + 1), qpos), -1: device(wrap(kpos - 1), qpos)}
    q_near = {1: device(kpos, wrap(qpos + 1)), -1: device(kpos, wrap(qpos - 1))}

    barrier = pltpu.get_barrier_semaphore()
    for near in (*k_near.values(), *q_near.values()):
        pl.semaphore_signal(barrier, inc=1, device_id={"tm": near}, device_id_type=MESH)
    for step in range(1, PEERS):
        pl.semaphore_signal(
            barrier, inc=1, device_id={"head": lax.rem(head + step, PEERS)}, device_id_type=MESH
        )

    own = {"k": k_ref, "v": v_ref, "q": q_ref}
    whole = {"k": k_all, "v": v_all, "q": q_all}
    position = {"k": kpos, "v": kpos, "q": qpos}
    nearby = {"k": k_near, "v": k_near, "q": q_near}
    legs = [(name, way, hop) for name in "kvq" for way in (1, -1) for hop in range(1, 4)]
    legs += [("k", 1, 4), ("v", -1, 4), ("q", 1, 4)]
    slot = {leg: number for number, leg in enumerate(legs)}

    def leg_copy(h, leg, arriving):
        name, way, hop = leg
        block = wrap(position[name] - way * (hop if arriving else hop - 1))
        there = whole[name].at[h, block]
        if hop == 1 and not arriving:
            here = own[name].at[:, pl.ds(h * HD, HD)]
        else:
            here = there
        return pltpu.make_async_remote_copy(
            src_ref=here,
            dst_ref=there,
            send_sem=g_send.at[h, slot[leg]],
            recv_sem=g_recv.at[h, slot[leg]],
            device_id={"tm": nearby[name][way]},
            device_id_type=MESH,
        )

    def send_hop(h, hop):
        for leg in legs:
            if leg[2] == hop:
                leg_copy(h, leg, False).start()

    def wait_hop(h, hop):
        for leg in legs:
            if leg[2] == hop:
                leg_copy(h, leg, True).wait_recv()

    def relay(h, hop):
        for leg in legs:
            if leg[2] == hop:
                leg_copy(h, leg, True).wait_recv()
                onward = (leg[0], leg[1], hop + 1)
                if onward in slot:
                    leg_copy(h, onward, False).start()

    def place(j):
        return wrap(qpos + jnp.where(lax.rem(j, 2) == 1, lax.div(7 - j, 2), lax.div(j + 8, 2)))

    pl.semaphore_wait(barrier, 4 + PEERS - 1)
    send_hop(0, 1)
    send_hop(1, 1)

    for h in range(HEADS_DEV):
        columns = slice(h * HD, (h + 1) * HD)
        k_all[h, kpos] = k_ref[:, columns]
        v_all[h, kpos] = v_ref[:, columns]
        q_all[h, qpos] = q_ref[:, columns]
        gains[h] = jnp.broadcast_to(gain_ref[columns][None, :], (8, HD))
        for first in range(2):
            inbox[h, first, :ROWS, :] = jnp.zeros((ROWS, 2 * HD), BF)
            stat_row = lax.broadcasted_iota(jnp.int32, (STAT, 2 * HD), 0)
            inbox[h, first, ROWS:, :] = jnp.where(
                (stat_row == 0) | (stat_row == 3), F32(EMPTY), F32(0.0)
            ).astype(BF)
    gap_sum[...] = jnp.zeros((ROWS, HD), F32)

    def set_bias(j, carry):
        q_group = group_ref[device(kpos, place(j))]
        block_of = lax.div(lax.broadcasted_iota(jnp.int32, (8, KEYS), 1), ROWS)
        row = jnp.zeros((8, KEYS), F32)
        for b in range(RING):
            keep = mask_ref[q_group, group_ref[device(b, qpos)]]
            row = jnp.where(block_of == b, jnp.where(keep == 1, F32(0.0), F32(EMPTY)), row)
        bias[j] = row
        return carry

    lax.fori_loop(0, RING, set_bias, 0)

    relay(0, 1)
    relay(1, 1)
    relay(0, 2)
    relay(1, 2)
    send_hop(2, 1)
    relay(0, 3)
    relay(1, 3)
    wait_hop(0, 4)

    def scores(h, j, score):
        queries = q_all[h, place(j)]
        gain = gains[h][0:1, :]
        teacher = (queries.astype(F32) * gain).astype(BF)
        both = jnp.concatenate([queries, teacher], axis=0)
        keys = k_all[h].reshape(KEYS, HD)
        score[...] = lax.dot_general(both, keys, NT, preferred_element_type=F32)

    def mix(h, j, score):
        s = jnp.concatenate([score[:ROWS, :] + bias[j][0:1, :], score[ROWS:, :]], axis=0)
        largest = jnp.max(s, axis=-1, keepdims=True)
        weight = jnp.exp2((s - largest) * SCALE).astype(BF)
        right = jnp.concatenate(
            [v_all[h].reshape(KEYS, HD), jnp.ones((KEYS, HD), BF)], axis=1
        )
        mixed = jnp.dot(weight, right, preferred_element_type=F32)
        denom = mixed[:, HD:]
        part[h, j] = mixed[:, :HD] / denom
        lse[h, j] = largest * SCALE + jnp.log2(denom)

    def unit(u):
        later = u - RING
        h = jnp.where(u < RING, 0, 1 + lax.rem(later + 2, 2))
        j = jnp.where(u < RING, u, lax.div(later, 2))
        return h, j

    stat_lane = lax.broadcasted_iota(jnp.int32, (ROWS, HD), 1)
    pick = lax.broadcasted_iota(jnp.int32, (STAT, HD), 0)
    diagonal = (pick == lax.broadcasted_iota(jnp.int32, (STAT, HD), 1)).astype(F32).astype(BF)
    spread = [
        ((pick >= 3 * i) & (pick < 3 * i + 3)).astype(F32).astype(BF) for i in range(2)
    ]

    def merge(h, box, i, out, log):
        came = inbox[h, box, :ROWS, i * HD:(i + 1) * HD].astype(F32)
        stat = inbox[h, box, ROWS:, :]
        came_log = lax.dot_general(stat, spread[i], TN, preferred_element_type=F32)[:ROWS]
        ahead = log - came_log
        share = 1.0 / (1.0 + jnp.exp2(ahead))
        return (
            out + share * (came - out),
            jnp.maximum(log, came_log) + jnp.log2(1.0 + jnp.exp2(-jnp.abs(ahead))),
        )

    def message(h, j, way, arriving):
        box = inbox.at[h, j + 2]
        return pltpu.make_async_remote_copy(
            src_ref=box if arriving else outbox.at[h, j],
            dst_ref=box,
            send_sem=o_send.at[h, j],
            recv_sem=o_recv.at[h, j],
            device_id={"tm": jnp.where(lax.rem(j, 2) == 1, q_near[1], q_near[-1])},
            device_id_type=MESH,
        )

    def pass_on(h, j):
        @pl.when(j >= 2)
        def _():
            message(h, j - 2, None, True).wait_recv()

        packed = jnp.zeros((ROWS, HD), F32)
        for i in range(2):
            out, log = merge(
                h, j, i, part[h, j, i * ROWS:(i + 1) * ROWS, :], lse[h, j, i * ROWS:(i + 1) * ROWS, :]
            )
            outbox[h, j, :ROWS, i * HD:(i + 1) * HD] = out.astype(BF)
            rest = log
            for piece in range(3):
                rounded = rest.astype(BF).astype(F32)
                packed = jnp.where(stat_lane == 3 * i + piece, rounded, packed)
                rest = rest - rounded
        packed = jnp.concatenate([packed, jnp.zeros((2 * HD - ROWS, HD), F32)], axis=0).astype(BF)
        outbox[h, j, ROWS:, :] = lax.dot_general(
            diagonal, packed, NT, preferred_element_type=F32
        ).astype(BF)
        message(h, j, None, False).start()

    def work(g, last=False):
        u = 2 * g
        h0, j0 = unit(u)
        h1, j1 = unit(u + 1)
        scores(h1, j1, score1)
        mix(h0, j0, score0)
        if not last:
            h2, j2 = unit(u + 2)
            scores(h2, j2, score0)
        mix(h1, j1, score1)

    scores(0, 0, score0)

    def turn(g, carry):
        for when, hop in ((0, 1), (1, 2), (2, 3)):
            @pl.when(g == when)
            def _(hop=hop):
                relay(2, hop)

        @pl.when(g == 3)
        def _():
            wait_hop(1, 4)
            wait_hop(2, 4)

        work(g)

        @pl.when((g >= 2) & (g <= 8))
        def _():
            pass_on(0, g - 2)

        @pl.when(g >= 4)
        def _():
            pass_on(1, g - 4)
            pass_on(2, g - 4)

        return carry

    lax.fori_loop(0, UNITS // 2 - 1, turn, 0)
    work(jnp.int32(UNITS // 2 - 1), last=True)

    for h in range(HEADS_DEV):
        message(h, 5, None, True).wait_recv()
        message(h, 6, None, True).wait_recv()
        final = []
        for i in range(2):
            out, log = merge(
                h, 7, i,
                part[h, 7, i * ROWS:(i + 1) * ROWS, :], lse[h, 7, i * ROWS:(i + 1) * ROWS, :],
            )
            out, log = merge(h, 8, i, out, log)
            final.append(out.astype(BF))
        s_out[:, h * HD:(h + 1) * HD] = final[0]
        t_out[:, h * HD:(h + 1) * HD] = final[1]
        apart = final[1].astype(F32) - final[0].astype(F32)
        gap_sum[...] += apart * apart

    tall = jnp.concatenate([gap_sum[...], jnp.zeros((2 * HD - ROWS, HD), F32)], axis=0)
    gap_in[head] = lax.dot_general(
        jnp.ones((8, HD), F32), tall, NT, preferred_element_type=F32,
        precision=lax.Precision.HIGHEST,
    )

    def gap_copy(step, arriving):
        other = lax.rem(head + (PEERS - step if arriving else step), PEERS)
        box = gap_in.at[other if arriving else head]
        return pltpu.make_async_remote_copy(
            src_ref=box,
            dst_ref=box,
            send_sem=d_send.at[step - 1],
            recv_sem=d_recv.at[step - 1],
            device_id={"head": other},
            device_id_type=MESH,
        )

    for step in range(1, PEERS):
        gap_copy(step, False).start()
    for h in range(HEADS_DEV):
        for leg in legs:
            leg_copy(h, leg, False).wait_send()
        for j in range(RING - 1):
            message(h, j, None, False).wait_send()
    for step in range(1, PEERS):
        gap_copy(step, True).wait_recv()
    total = gap_in[0]
    for peer in range(1, PEERS):
        total = total + gap_in[peer]
    gap_out[...] = total / F32(PEERS * HEADS_DEV * HD)
    for step in range(1, PEERS):
        gap_copy(step, False).wait_send()


def on_device(queries, keys, values, block_group, group_mask, teacher_gain):
    vmem = pl.BlockSpec(memory_space=pltpu.VMEM)
    smem = pl.BlockSpec(memory_space=pltpu.SMEM)
    legs = 21
    student, teacher, gap = pl.pallas_call(
        kernel,
        out_shape=(
            jax.ShapeDtypeStruct((ROWS, HEADS_DEV * HD), BF),
            jax.ShapeDtypeStruct((ROWS, HEADS_DEV * HD), BF),
            jax.ShapeDtypeStruct((8, 2 * HD), F32),
        ),
        in_specs=[vmem, vmem, vmem, smem, smem, vmem],
        out_specs=(vmem, vmem, vmem),
        scratch_shapes=[
            pltpu.VMEM((HEADS_DEV, RING, ROWS, HD), BF),
            pltpu.VMEM((HEADS_DEV, RING, ROWS, HD), BF),
            pltpu.VMEM((HEADS_DEV, RING, ROWS, HD), BF),
            pltpu.VMEM((RING, 8, KEYS), F32),
            pltpu.VMEM((HEADS_DEV, 8, HD), F32),
            pltpu.VMEM((2 * ROWS, KEYS), F32),
            pltpu.VMEM((2 * ROWS, KEYS), F32),
            pltpu.VMEM((HEADS_DEV, RING, 2 * ROWS, HD), F32),
            pltpu.VMEM((HEADS_DEV, RING, 2 * ROWS, HD), F32),
            pltpu.VMEM((HEADS_DEV, RING + 1, ROWS + STAT, 2 * HD), BF),
            pltpu.VMEM((HEADS_DEV, RING - 1, ROWS + STAT, 2 * HD), BF),
            pltpu.VMEM((ROWS, HD), F32),
            pltpu.VMEM((PEERS, 8, 2 * HD), F32),
            pltpu.SemaphoreType.DMA((HEADS_DEV, legs)),
            pltpu.SemaphoreType.DMA((HEADS_DEV, legs)),
            pltpu.SemaphoreType.DMA((HEADS_DEV, RING - 1)),
            pltpu.SemaphoreType.DMA((HEADS_DEV, RING - 1)),
            pltpu.SemaphoreType.DMA((PEERS - 1,)),
            pltpu.SemaphoreType.DMA((PEERS - 1,)),
        ],
        compiler_params=pltpu.CompilerParams(
            collective_id=0, has_side_effects=True, vmem_limit_bytes=48 * 2**20
        ),
    )(queries, keys, values, block_group, group_mask, teacher_gain)
    return student, teacher, gap[0, :ROWS]


def solution(mesh):
    placed = (P("tm", "head"), P("tm", "head"), P("tm", "head"), P(), P(), P("head"))
    return jax.shard_map(
        on_device,
        mesh=mesh,
        in_specs=placed,
        out_specs=(P("tm", "head"), P("tm", "head"), P("tm")),
        check_vma=False,
    )
```

time: 363 us -> 78.4 us (0.22)
  the two profiles are of different devices: /device:TPU:32 before, /device:TPU:1 now
where the time goes in v1:
time: 78.4 us; the launch traced here: 78.1 us
  Pallas kernels  70.9 us (90%)
  local copies, waits for them, and re-layouts  6.57 us (8%)
    pallas_call x1, Pallas kernels, on_device(): pl.pallas_call(kernel, out_shape=(jax.ShapeDtypeStruct((ROWS, HEADS_DEV *...  70.9 us
    unnamed x14, local copies, waits for them, and re-layouts  6.01 us

profile of v1, /device:TPU:1, one launch (start us, length us, event | category | flops | bytes accessed | tf_op | source)
XLA Modules:
  0.0 78.1 jit_solution(1695043000356144856)
XLA Ops:
  0.6 0.0 copy-start
  0.6 0.9 %copy-done = bf16[160,384]{1,0:T(8,128)(2,1)S(1)} copy-done((bf16[160,384]{1,0:T(8,128)(2,1)S(1)}, bf16[160,384]{1,0:T(8,128)(2,1)}, u32[]{:S(2)}) %copy-start) | copy-done | bytes 122904
  1.5 0.0 copy-start.1
  1.5 0.9 %copy-done.1 = bf16[160,384]{1,0:T(8,128)(2,1)S(1)} copy-done((bf16[160,384]{1,0:T(8,128)(2,1)S(1)}, bf16[160,384]{1,0:T(8,128)(2,1)}, u32[]{:S(2)}) %copy-start.1) | copy-done | bytes 122904
  2.4 0.0 copy-start.2
  2.4 0.9 %copy-done.2 = bf16[160,384]{1,0:T(8,128)(2,1)S(1)} copy-done((bf16[160,384]{1,0:T(8,128)(2,1)S(1)}, bf16[160,384]{1,0:T(8,128)(2,1)}, u32[]{:S(2)}) %copy-start.2) | copy-done | bytes 122904
  3.3 0.0 copy-start.3
  3.3 0.7 copy-done.3
  4.0 0.0 copy-start.4
  4.0 0.7 copy-done.4
  4.7 0.0 copy-start.5
  4.7 0.7 copy-done.5
  5.4 70.9 %shard_map.85 = (bf16[160,384]{1,0:T(8,128)(2,1)S(1)}, bf16[160,384]{1,0:T(8,128)(2,1)S(1)}, f32[8,256]{1,0:T(8,128)S(1)}) custom-call(bf16[160,384]{1,0:T(8,128)(2,1)S(1)} %copy-done, bf16[160,384]{1,0:T(8,128)(2,1)S(1)} %copy-done.1, bf16[160,384]{1,0:T(8,128)(2,1)S(1)} %copy-done.2, s32[64]{0:T(128)S(1)} %copy-done.5, s32[4,4]{1,0:T(4,128)S(1)} %copy-done.3, ...), custom_call_target="tpu_custom_call" | custom-call | tf_op jit(solution)/shard_map/pallas_call | solution.py:315
  76.3 0.6 slice.3
  76.8 0.6 copy.11
  77.5 0.6 copy.12
Async XLA Ops:
  0.6 0.9 %copy-start = (bf16[160,384]{1,0:T(8,128)(2,1)S(1)}, bf16[160,384]{1,0:T(8,128)(2,1)}, u32[]{:S(2)}) copy-start(bf16[160,384]{1,0:T(8,128)(2,1)} %q_ref.1) | copy-start | bytes 368644
  1.5 0.9 %copy-start.1 = (bf16[160,384]{1,0:T(8,128)(2,1)S(1)}, bf16[160,384]{1,0:T(8,128)(2,1)}, u32[]{:S(2)}) copy-start(bf16[160,384]{1,0:T(8,128)(2,1)} %k_ref.1) | copy-start | bytes 368644
  2.4 0.9 %copy-start.2 = (bf16[160,384]{1,0:T(8,128)(2,1)S(1)}, bf16[160,384]{1,0:T(8,128)(2,1)}, u32[]{:S(2)}) copy-start(bf16[160,384]{1,0:T(8,128)(2,1)} %v_ref.1) | copy-start | bytes 368644
  3.3 0.7 copy-start.3
  4.0 0.7 copy-start.4
  4.7 0.7 copy-start.5

commit v2 on v1

v2 whole, which is shorter than its diff:
```python
import functools
import math

import jax
import jax.numpy as jnp
from jax import lax
from jax.experimental import pallas as pl
from jax.experimental.pallas import tpu as pltpu
from jax.sharding import PartitionSpec as P

HD = 128
RING = 8
HEADS_DEV = 3
PEERS = 8
ROWS = 160
STAT = 16
KEYS = RING * ROWS
UNITS = RING * HEADS_DEV
SCALE = math.log2(math.e) / math.sqrt(HD)
EMPTY = -(2.0**100)
MESH = pl.DeviceIdType.MESH
NT = (((1,), (1,)), ((), ()))
TN = (((0,), (0,)), ((), ()))
BF = jnp.bfloat16
F32 = jnp.float32


def kernel(
    q_ref, k_ref, v_ref, group_ref, mask_ref, gain_ref,
    s_out, t_out, gap_out,
    kv_all, q_all, group_all, mask_all, gain_all, bias, gains, score0, score1, inbox, outbox, gap_sum, gap_in,
    l_sem, g_send, g_recv, o_send, o_recv, d_send, d_recv,
):
    tm = lax.axis_index("tm")
    head = lax.axis_index("head")
    core = lax.rem(head, 2)
    zpos, ypos = lax.div(tm, RING), lax.rem(tm, RING)
    kpos = jnp.where(core == 0, zpos, ypos)
    qpos = jnp.where(core == 0, ypos, zpos)

    def device(kp, qp):
        return jnp.where(core == 0, kp * RING + qp, qp * RING + kp)

    def wrap(x):
        return lax.rem(x + 2 * RING, RING)

    def k_device(shift):
        return device(wrap(kpos + shift), qpos)

    def q_device(shift):
        return device(kpos, wrap(qpos + shift))

    sources = (q_ref, k_ref, v_ref)
    own_copies = []
    for h in range(HEADS_DEV):
        places = (q_all.at[0, h], kv_all.at[h, 0, 0], kv_all.at[h, 0, 1])
        for i, (source, place) in enumerate(zip(sources, places)):
            own_copies.append(
                pltpu.make_async_copy(source.at[:, pl.ds(h * HD, HD)], place, l_sem.at[h, i])
            )
    small = ((group_ref, group_all), (mask_ref, mask_all), (gain_ref, gain_all))
    small_copies = [
        pltpu.make_async_copy(source, place, l_sem.at[HEADS_DEV, i])
        for i, (source, place) in enumerate(small)
    ]
    for copy in own_copies + small_copies:
        copy.start()

    barrier = pltpu.get_barrier_semaphore()
    nears = [k_device(1), k_device(-1)] + [q_device(shift) for shift in (1, -1, 2, -2)]
    for near in nears:
        pl.semaphore_signal(barrier, inc=1, device_id={"tm": near}, device_id_type=MESH)
    for step in range(1, PEERS):
        pl.semaphore_signal(
            barrier, inc=1, device_id={"head": lax.rem(head + step, PEERS)}, device_id_type=MESH
        )

    def number(way, far):
        return 0 if far == 0 else 7 if far == 4 else 2 * far - (way > 0)

    def offset(k):
        return jnp.where(lax.rem(k, 2) == 1, lax.div(k + 1, 2), -lax.div(k, 2))

    legs = [(what, way, hop) for hop in (1, 2, 3) for what in (0, "q", 1, 2) for way in (1, -1)]
    legs += [(0, 1, 4), (0, -1, 4), ("q", 1, 4), (1, 1, 4), (1, -1, 4), (2, 1, 4), (2, -1, 4)]

    def leg_copy(leg):
        what, way, hop = leg
        here, there = number(-way, hop - 1), number(-way, hop)
        if what == "q":
            ends = q_all.at[here], q_all.at[there]
            near = q_device(way)
        else:
            ends = kv_all.at[what, here], kv_all.at[what, there]
            if hop == 4:
                half = 0 if way == 1 else 1
                ends = tuple(end.at[half] for end in ends)
            near = k_device(way)
        i = legs.index(leg)
        return pltpu.make_async_remote_copy(
            src_ref=ends[0],
            dst_ref=ends[1],
            send_sem=g_send.at[i],
            recv_sem=g_recv.at[i],
            device_id={"tm": near},
            device_id_type=MESH,
        )

    def relay(hop):
        for leg in legs:
            if leg[2] == hop:
                leg_copy(leg).wait_recv()
                onward = (leg[0], leg[1], hop + 1)
                if onward in legs:
                    leg_copy(onward).start()

    def wait_last(what):
        for leg in legs:
            if leg[0] == what and leg[2] == 4:
                leg_copy(leg).wait_recv()

    pl.semaphore_wait(barrier, len(nears) + PEERS - 1)
    for copy in own_copies:
        copy.wait()
    for leg in legs:
        if leg[2] == 1:
            leg_copy(leg).start()

    for copy in small_copies:
        copy.wait()
    for h in range(HEADS_DEV):
        gains[h] = jnp.broadcast_to(gain_all[h * HD:(h + 1) * HD][None, :], (8, HD))
    gap_sum[...] = jnp.zeros((ROWS, HD), F32)

    def set_bias(k, carry):
        q_group = group_all[device(kpos, wrap(qpos + offset(k)))]
        block_of = lax.div(lax.broadcasted_iota(jnp.int32, (8, KEYS), 1), ROWS)
        row = jnp.zeros((8, KEYS), F32)
        for i in range(RING):
            step = (i + 1) // 2 if i % 2 else -(i // 2)
            keep = mask_all[q_group, group_all[k_device(step)]]
            row = jnp.where(block_of == i, jnp.where(keep == 1, F32(0.0), F32(EMPTY)), row)
        bias[k] = row
        return carry

    lax.fori_loop(0, RING, set_bias, 0)

    for hop in (1, 2, 3):
        relay(hop)
    wait_last(0)

    def scores(h, k, score):
        queries = q_all[k, h]
        gain = gains[h][0:1, :]
        teacher = (queries.astype(F32) * gain).astype(BF)
        both = jnp.concatenate([queries, teacher], axis=0)
        keys = kv_all[h, :, 0].reshape(KEYS, HD)
        score[...] = lax.dot_general(both, keys, NT, preferred_element_type=F32)

    def mix(h, k, score):
        s = jnp.concatenate([score[:ROWS, :] + bias[k][0:1, :], score[ROWS:, :]], axis=0)
        shift = jnp.max(s, axis=-1, keepdims=True).astype(BF).astype(F32)
        weight = jnp.exp2((s - shift) * SCALE).astype(BF)
        right = jnp.concatenate(
            [kv_all[h, :, 1].reshape(KEYS, HD), jnp.ones((KEYS, HD), BF)], axis=1
        )
        mixed = jnp.dot(weight, right, preferred_element_type=F32)
        shift = jnp.broadcast_to(shift, (2 * ROWS, HD))
        halves = (slice(0, ROWS), slice(ROWS, 2 * ROWS))
        pack(h, k, [(mixed[half, :HD], shift[half], mixed[half, HD:]) for half in halves])

    def unit(u):
        v = u - 7
        h = jnp.where(
            v < 0, 0,
            jnp.where(
                v >= 14, v - 14,
                jnp.where((v < 3) | (v == 6) | (v == 7) | (v == 10) | (v == 11), 1, 2),
            ),
        )
        k = jnp.where(
            v < 0, u + 1,
            jnp.where(
                v >= 14, 0,
                jnp.where(v < 3, 7 - v, jnp.where(v < 8, 10 - v, jnp.where(v < 12, 12 - v, 14 - v))),
            ),
        )
        return h, k

    stat_lane = lax.broadcasted_iota(jnp.int32, (ROWS, HD), 1)
    stat_row = lax.broadcasted_iota(jnp.int32, (STAT, 2 * HD), 0)
    sum_side = jnp.where(lax.broadcasted_iota(jnp.int32, (STAT, 2 * HD), 1) >= HD, 1, 0)
    wanted = [lax.div(stat_row - 3 * i + 1, 2) for i in range(2)]
    spread = [
        jnp.where((wanted[i] == sum_side) & (stat_row >= 3 * i), F32(1.0), F32(0.0)).astype(BF)
        for i in range(2)
    ]

    def unpack(box, h, k, i):
        out = box[h, k, :ROWS, i * HD:(i + 1) * HD].astype(F32)
        stat = lax.dot_general(
            box[h, k, ROWS:, :], spread[i], TN, preferred_element_type=F32
        )[:ROWS]
        return out, stat[:, :HD], stat[:, HD:]

    def merge(parts):
        top = parts[0][1]
        for _, shift, _ in parts[1:]:
            top = jnp.maximum(top, shift)
        mixed = 0.0
        total = 0.0
        for out, shift, weight in parts:
            share = jnp.exp2((shift - top) * SCALE)
            mixed = mixed + share * out
            total = total + share * weight
        return mixed, top, total

    def message(h, k, shift):
        return pltpu.make_async_remote_copy(
            src_ref=outbox.at[h, k],
            dst_ref=inbox.at[h, k],
            send_sem=o_send.at[h, k],
            recv_sem=o_recv.at[h, k],
            device_id={"tm": q_device(shift)},
            device_id_type=MESH,
        )

    def arrived(h, k):
        message(h, k, 1).wait_recv()

    def pack(h, k, parts):
        packed = jnp.zeros((ROWS, HD), F32)
        for i, (out, shift, weight) in enumerate(parts):
            outbox[h, k, :ROWS, i * HD:(i + 1) * HD] = out.astype(BF)
            upper = weight.astype(BF).astype(F32)
            for piece, value in enumerate((shift, upper, weight - upper)):
                packed = jnp.where(stat_lane == 3 * i + piece, value, packed)
        packed = jnp.concatenate([packed, jnp.zeros((2 * HD - ROWS, HD), F32)], axis=0)
        outbox[h, k, ROWS:, :] = packed.T[:STAT].astype(BF)

    def pass_on(h, k, shift, others):
        for other in others:
            arrived(h, other)
        pack(h, k, [
            merge([unpack(outbox, h, k, i)] + [unpack(inbox, h, other, i) for other in others])
            for i in range(2)
        ])
        message(h, k, shift).start()

    def work(g, last=False):
        h0, k0 = unit(2 * g)
        h1, k1 = unit(2 * g + 1)
        scores(h1, k1, score1)
        mix(h0, k0, score0)
        if not last:
            h2, k2 = unit(2 * g + 2)
            scores(h2, k2, score0)
        mix(h1, k1, score1)
        return (h0, k0), (h1, k1)

    scores(0, 1, score0)

    def turn(g, carry):
        for when, what in ((2, "q"), (3, 1), (4, 2)):
            @pl.when(g == when)
            def _(what=what):
                wait_last(what)

        done = work(g)
        for h, k in done:
            @pl.when((k != 0) & (k != 3) & (k != 4))
            def _(h=h, k=k):
                message(h, k, jnp.where(k == 7, 2, jnp.where(lax.rem(k, 2) == 1, 1, -1))).start()

        @pl.when((g == 5) | (g == 7) | (g == 8))
        def _():
            pass_on(jnp.where(g == 5, 0, g - 6), 4, -2, (6,))

        @pl.when((g == 6) | (g == 7) | (g == 9))
        def _():
            pass_on(jnp.where(g == 6, 0, jnp.where(g == 7, 1, 2)), 3, 2, (5, 7))

        return carry

    lax.fori_loop(0, UNITS // 2 - 1, turn, 0)
    work(jnp.int32(UNITS // 2 - 1), last=True)

    for h in range(HEADS_DEV):
        for k in (1, 2, 3, 4):
            arrived(h, k)
        final = []
        for i in range(2):
            out, _, total = merge(
                [unpack(outbox, h, 0, i)] + [unpack(inbox, h, k, i) for k in (1, 2, 3, 4)]
            )
            final.append((out / total).astype(BF))
        s_out[:, h * HD:(h + 1) * HD] = final[0]
        t_out[:, h * HD:(h + 1) * HD] = final[1]
        apart = final[1].astype(F32) - final[0].astype(F32)
        gap_sum[...] += apart * apart

    tall = jnp.concatenate([gap_sum[...], jnp.zeros((2 * HD - ROWS, HD), F32)], axis=0)
    gap_in[head] = jnp.broadcast_to(jnp.sum(tall.T, axis=0, keepdims=True), (8, 2 * HD))

    def gap_copy(step, arriving):
        other = lax.rem(head + (PEERS - step if arriving else step), PEERS)
        box = gap_in.at[other if arriving else head]
        return pltpu.make_async_remote_copy(
            src_ref=box,
            dst_ref=box,
            send_sem=d_send.at[step - 1],
            recv_sem=d_recv.at[step - 1],
            device_id={"head": other},
            device_id_type=MESH,
        )

    for step in range(1, PEERS):
        gap_copy(step, False).start()
    for leg in legs:
        leg_copy(leg).wait_send()
    for h in range(HEADS_DEV):
        for k in range(1, RING):
            message(h, k, 1).wait_send()
    for step in range(1, PEERS):
        gap_copy(step, True).wait_recv()
    total = gap_in[0]
    for peer in range(1, PEERS):
        total = total + gap_in[peer]
    gap_out[...] = total / F32(PEERS * HEADS_DEV * HD)
    for step in range(1, PEERS):
        gap_copy(step, False).wait_send()


def on_device(queries, keys, values, block_group, group_mask, teacher_gain):
    vmem = pl.BlockSpec(memory_space=pltpu.VMEM)
    outside = pl.BlockSpec(memory_space=pltpu.HBM)
    legs = 31
    student, teacher, gap = pl.pallas_call(
        kernel,
        out_shape=(
            jax.ShapeDtypeStruct((ROWS, HEADS_DEV * HD), BF),
            jax.ShapeDtypeStruct((ROWS, HEADS_DEV * HD), BF),
            jax.ShapeDtypeStruct((8, 2 * HD), F32),
        ),
        in_specs=[outside] * 6,
        out_specs=(vmem, vmem, vmem),
        scratch_shapes=[
            pltpu.VMEM((HEADS_DEV, RING, 2, ROWS, HD), BF),
            pltpu.VMEM((RING, HEADS_DEV, ROWS, HD), BF),
            pltpu.SMEM(block_group.shape, jnp.int32),
            pltpu.SMEM(group_mask.shape, jnp.int32),
            pltpu.VMEM(teacher_gain.shape, F32),
            pltpu.VMEM((RING, 8, KEYS), F32),
            pltpu.VMEM((HEADS_DEV, 8, HD), F32),
            pltpu.VMEM((2 * ROWS, KEYS), F32),
            pltpu.VMEM((2 * ROWS, KEYS), F32),
            pltpu.VMEM((HEADS_DEV, RING, ROWS + STAT, 2 * HD), BF),
            pltpu.VMEM((HEADS_DEV, RING, ROWS + STAT, 2 * HD), BF),
            pltpu.VMEM((ROWS, HD), F32),
            pltpu.VMEM((PEERS, 8, 2 * HD), F32),
            pltpu.SemaphoreType.DMA((HEADS_DEV + 1, 3)),
            pltpu.SemaphoreType.DMA((legs,)),
            pltpu.SemaphoreType.DMA((legs,)),
            pltpu.SemaphoreType.DMA((HEADS_DEV, RING)),
            pltpu.SemaphoreType.DMA((HEADS_DEV, RING)),
            pltpu.SemaphoreType.DMA((PEERS - 1,)),
            pltpu.SemaphoreType.DMA((PEERS - 1,)),
        ],
        compiler_params=pltpu.CompilerParams(
            collective_id=0, has_side_effects=True, vmem_limit_bytes=64 * 2**20
        ),
    )(queries, keys, values, block_group, group_mask, teacher_gain)
    return student, teacher, gap[0, :ROWS]


def solution(mesh):
    placed = (P("tm", "head"), P("tm", "head"), P("tm", "head"), P(), P(), P("head"))
    return jax.shard_map(
        on_device,
        mesh=mesh,
        in_specs=placed,
        out_specs=(P("tm", "head"), P("tm", "head"), P("tm")),
        check_vma=False,
    )
```

time: 78.4 us -> 67.1 us (0.86)
  Pallas kernels: 70.9 us -> 62.7 us
  local copies, waits for them, and re-layouts: 6.57 us -> 3.51 us
    pallas_call x1, Pallas kernels: 70.9 us -> 62.7 us  [on_device(): pl.pallas_call(kernel, out_shape=(jax.ShapeDtypeStruct((ROWS, HEADS_DEV *...]
    unnamed x14 -> x4, local copies, waits for them, and re-layouts: 6.01 us -> 2.25 us
where the time goes in v2:
time: 67.1 us; the launch traced here: 66.9 us
  Pallas kernels  62.7 us (93%)
  local copies, waits for them, and re-layouts  3.51 us (5%)
    pallas_call x1, Pallas kernels, on_device(): pl.pallas_call(kernel, out_shape=(jax.ShapeDtypeStruct((ROWS, HEADS_DEV *...  62.7 us
    unnamed x4, local copies, waits for them, and re-layouts  2.25 us

profile of v2, /device:TPU:1, one launch (start us, length us, event | category | flops | bytes accessed | tf_op | source)
XLA Modules:
  0.0 66.9 jit_solution(10371423166292861668)
XLA Ops:
  0.6 62.7 %shard_map.85 = (bf16[160,384]{1,0:T(8,128)(2,1)}, bf16[160,384]{1,0:T(8,128)(2,1)}, f32[8,256]{1,0:T(8,128)}) custom-call(bf16[160,384]{1,0:T(8,128)(2,1)} %q_ref.1, bf16[160,384]{1,0:T(8,128)(2,1)} %k_ref.1, bf16[160,384]{1,0:T(8,128)(2,1)} %v_ref.1, s32[64]{0:T(128)} %group_ref.1, s32[4,4]{1,0:T(4,128)} %mask_ref.1, f32[384]{0:T(512)} %gain_ref.1), custom_call_target="tpu_custom_call" | custom-call | tf_op jit(solution)/shard_map/pallas_call | solution.py:338
  63.4 1.3 %slice.3 = f32[1,160]{1,0:T(1,128)} slice(f32[8,256]{1,0:T(8,128)} %get-tuple-element.8), slice={[0:1], [0:160]} | slice | bytes 1280 | tf_op jit(solution)/shard_map/slice | solution.py:373
  64.6 0.0 copy-start
  64.6 1.6 %copy.11 = bf16[160,384]{1,0:T(8,128)(2,1)} copy(bf16[160,384]{1,0:T(8,128)(2,1)} %get-tuple-element.12) | data formatting | bytes 245760
  66.2 0.0 copy-done
  66.2 0.6 copy.12
Async XLA Ops:
  64.6 1.6 %copy-start = (bf16[160,384]{1,0:T(8,128)(2,1)S(1)}, bf16[160,384]{1,0:T(8,128)(2,1)}, u32[]{:S(2)}) copy-start(bf16[160,384]{1,0:T(8,128)(2,1)} %get-tuple-element.13) | copy-start | bytes 368644

commit v3 on v2

--- a/solution.py
+++ b/solution.py
@@ -27,9 +27,9 @@
 
 def kernel(
     q_ref, k_ref, v_ref, group_ref, mask_ref, gain_ref,
-    s_out, t_out, gap_out,
-    kv_all, q_all, group_all, mask_all, gain_all, bias, gains, score0, score1, inbox, outbox, gap_sum, gap_in,
-    l_sem, g_send, g_recv, o_send, o_recv, d_send, d_recv,
+    s_hbm, t_hbm, gap_hbm,
+    kv_all, q_all, group_all, mask_all, gain_all, bias, gains, score0, score1, s_out, t_out, gap_out, inbox, outbox, gap_sum, gap_in,
+    l_sem, w_sem, g_send, g_recv, o_send, o_recv, d_send, d_recv,
 ):
     tm = lax.axis_index("tm")
     head = lax.axis_index("head")
@@ -106,6 +106,26 @@
             device_id_type=MESH,
         )
 
+    def send_own(leg):
+        what, way, _ = leg
+        i = legs.index(leg)
+        if what == "q":
+            pieces = [(q_ref, h, q_all.at[number(-way, 1), h]) for h in range(HEADS_DEV)]
+        else:
+            pieces = [
+                (source, what, kv_all.at[what, number(-way, 1), half])
+                for half, source in enumerate((k_ref, v_ref))
+            ]
+        for source, h, place in pieces:
+            pltpu.make_async_remote_copy(
+                src_ref=source.at[:, pl.ds(h * HD, HD)],
+                dst_ref=place,
+                send_sem=g_send.at[i],
+                recv_sem=g_recv.at[i],
+                device_id={"tm": (q_device if what == "q" else k_device)(way)},
+                device_id_type=MESH,
+            ).start()
+
     def relay(hop):
         for leg in legs:
             if leg[2] == hop:
@@ -120,11 +140,9 @@
                 leg_copy(leg).wait_recv()
 
     pl.semaphore_wait(barrier, len(nears) + PEERS - 1)
-    for copy in own_copies:
-        copy.wait()
     for leg in legs:
         if leg[2] == 1:
-            leg_copy(leg).start()
+            send_own(leg)
 
     for copy in small_copies:
         copy.wait()
@@ -145,6 +163,8 @@
 
     lax.fori_loop(0, RING, set_bias, 0)
 
+    for copy in own_copies:
+        copy.wait()
     for hop in (1, 2, 3):
         relay(hop)
     wait_last(0)
@@ -170,19 +190,24 @@
         pack(h, k, [(mixed[half, :HD], shift[half], mixed[half, HD:]) for half in halves])
 
     def unit(u):
-        v = u - 7
+        far = u - 3
+        middle = u - 9
+        near = u - 15
+        last = lax.rem(far + 3, 3)
         h = jnp.where(
-            v < 0, 0,
+            u < 3, 0,
             jnp.where(
-                v >= 14, v - 14,
-                jnp.where((v < 3) | (v == 6) | (v == 7) | (v == 10) | (v == 11), 1, 2),
+                u < 9, 1 + lax.div(far, 3),
+                jnp.where(u < 15, lax.div(middle, 2), jnp.where(u < 21, lax.div(near, 2), u - 21)),
             ),
         )
         k = jnp.where(
-            v < 0, u + 1,
+            u < 3, 5 + u,
             jnp.where(
-                v >= 14, 0,
-                jnp.where(v < 3, 7 - v, jnp.where(v < 8, 10 - v, jnp.where(v < 12, 12 - v, 14 - v))),
+                u < 9, jnp.where(last == 0, 7, 4 + last),
+                jnp.where(
+                    u < 15, 3 + lax.rem(middle, 2), jnp.where(u < 21, 1 + lax.rem(near, 2), 0)
+                ),
             ),
         )
         return h, k
@@ -258,46 +283,59 @@
         mix(h1, k1, score1)
         return (h0, k0), (h1, k1)
 
-    scores(0, 1, score0)
+    scores(0, 5, score0)
+
+    joins = ((3, (5,), 4, (0, 2)), (3, (5, 7), 4, (1,)), (4, (6, 7), 5, (0, 2)), (4, (6,), 5, (1,)))
+    joins += ((1, (3,), 7, (0, 1, 2)), (2, (4,), 8, (0, 1, 2)))
 
     def turn(g, carry):
-        for when, what in ((2, "q"), (3, 1), (4, 2)):
+        for when, what in ((0, "q"), (1, 1), (2, 2)):
             @pl.when(g == when)
             def _(what=what):
                 wait_last(what)
 
-        done = work(g)
-        for h, k in done:
-            @pl.when((k != 0) & (k != 3) & (k != 4))
+        for h, k in work(g):
+            @pl.when(k >= 5)
             def _(h=h, k=k):
-                message(h, k, jnp.where(k == 7, 2, jnp.where(lax.rem(k, 2) == 1, 1, -1))).start()
-
-        @pl.when((g == 5) | (g == 7) | (g == 8))
-        def _():
-            pass_on(jnp.where(g == 5, 0, g - 6), 4, -2, (6,))
-
-        @pl.when((g == 6) | (g == 7) | (g == 9))
-        def _():
-            pass_on(jnp.where(g == 6, 0, jnp.where(g == 7, 1, 2)), 3, 2, (5, 7))
+                across = jnp.where(h == 1, 2, -2)
+                message(h, k, jnp.where(k == 7, across, jnp.where(k == 5, 1, -1))).start()
+
+        for k, others, first, heads in joins:
+            mine = g == first + heads[0]
+            for h in heads[1:]:
+                mine = mine | (g == first + h)
+
+            @pl.when(mine)
+            def _(k=k, others=others, first=first):
+                pass_on(g - first, k, 1 if k % 2 else -1, others)
 
         return carry
 
     lax.fori_loop(0, UNITS // 2 - 1, turn, 0)
     work(jnp.int32(UNITS // 2 - 1), last=True)
 
+    def written(h):
+        columns = pl.ds(h * HD, HD)
+        return [
+            pltpu.make_async_copy(held.at[:, columns], out.at[:, columns], w_sem.at[h, i])
+            for i, (held, out) in enumerate(((s_out, s_hbm), (t_out, t_hbm)))
+        ]
+
     for h in range(HEADS_DEV):
-        for k in (1, 2, 3, 4):
+        for k in (1, 2):
             arrived(h, k)
         final = []
         for i in range(2):
             out, _, total = merge(
-                [unpack(outbox, h, 0, i)] + [unpack(inbox, h, k, i) for k in (1, 2, 3, 4)]
+                [unpack(outbox, h, 0, i)] + [unpack(inbox, h, k, i) for k in (1, 2)]
             )
             final.append((out / total).astype(BF))
         s_out[:, h * HD:(h + 1) * HD] = final[0]
         t_out[:, h * HD:(h + 1) * HD] = final[1]
         apart = final[1].astype(F32) - final[0].astype(F32)
         gap_sum[...] += apart * apart
+        for copy in written(h):
+            copy.start()
 
     tall = jnp.concatenate([gap_sum[...], jnp.zeros((2 * HD - ROWS, HD), F32)], axis=0)
     gap_in[head] = jnp.broadcast_to(jnp.sum(tall.T, axis=0, keepdims=True), (8, 2 * HD))
@@ -327,8 +365,34 @@
     for peer in range(1, PEERS):
         total = total + gap_in[peer]
     gap_out[...] = total / F32(PEERS * HEADS_DEV * HD)
+    gap_copied = pltpu.make_async_copy(gap_out, gap_hbm, w_sem.at[HEADS_DEV, 0])
+    gap_copied.start()
+    for h in range(HEADS_DEV):
+        for copy in written(h):
+            copy.wait()
+    gap_copied.wait()
     for step in range(1, PEERS):
         gap_copy(step, False).wait_send()
+
+
+def hand_over(s_ref, t_ref, gap_ref, s_out, t_out, gap_out, held, gap_held, sem):
+    gap_in = pltpu.make_async_copy(gap_ref, gap_held, sem.at[2, 0])
+    ways = []
+    for i, (source, target) in enumerate(((s_ref, s_out), (t_ref, t_out))):
+        ways.append((
+            pltpu.make_async_copy(source, held.at[i], sem.at[i, 0]),
+            pltpu.make_async_copy(held.at[i], target, sem.at[i, 1]),
+        ))
+    for arrive, _ in ways:
+        arrive.start()
+    gap_in.start()
+    for arrive, leave in ways:
+        arrive.wait()
+        leave.start()
+    gap_in.wait()
+    gap_out[...] = gap_held[0:1, :ROWS]
+    for _, leave in ways:
+        leave.wait()
 
 
 def on_device(queries, keys, values, block_group, group_mask, teacher_gain):
@@ -343,7 +407,7 @@
             jax.ShapeDtypeStruct((8, 2 * HD), F32),
         ),
         in_specs=[outside] * 6,
-        out_specs=(vmem, vmem, vmem),
+        out_specs=(outside,) * 3,
         scratch_shapes=[
             pltpu.VMEM((HEADS_DEV, RING, 2, ROWS, HD), BF),
             pltpu.VMEM((RING, HEADS_DEV, ROWS, HD), BF),
@@ -354,11 +418,15 @@
             pltpu.VMEM((HEADS_DEV, 8, HD), F32),
             pltpu.VMEM((2 * ROWS, KEYS), F32),
             pltpu.VMEM((2 * ROWS, KEYS), F32),
+            pltpu.VMEM((ROWS, HEADS_DEV * HD), BF),
+            pltpu.VMEM((ROWS, HEADS_DEV * HD), BF),
+            pltpu.VMEM((8, 2 * HD), F32),
             pltpu.VMEM((HEADS_DEV, RING, ROWS + STAT, 2 * HD), BF),
             pltpu.VMEM((HEADS_DEV, RING, ROWS + STAT, 2 * HD), BF),
             pltpu.VMEM((ROWS, HD), F32),
             pltpu.VMEM((PEERS, 8, 2 * HD), F32),
             pltpu.SemaphoreType.DMA((HEADS_DEV + 1, 3)),
+            pltpu.SemaphoreType.DMA((HEADS_DEV + 1, 2)),
             pltpu.SemaphoreType.DMA((legs,)),
             pltpu.SemaphoreType.DMA((legs,)),
             pltpu.SemaphoreType.DMA((HEADS_DEV, RING)),
@@ -370,7 +438,23 @@
             collective_id=0, has_side_effects=True, vmem_limit_bytes=64 * 2**20
         ),
     )(queries, keys, values, block_group, group_mask, teacher_gain)
-    return student, teacher, gap[0, :ROWS]
+    student, teacher, gap = pl.pallas_call(
+        hand_over,
+        out_shape=(
+            jax.ShapeDtypeStruct(student.shape, BF),
+            jax.ShapeDtypeStruct(teacher.shape, BF),
+            jax.ShapeDtypeStruct((1, ROWS), F32),
+        ),
+        in_specs=[outside] * 3,
+        out_specs=(outside, outside, vmem),
+        scratch_shapes=[
+            pltpu.VMEM((2, ROWS, HEADS_DEV * HD), BF),
+            pltpu.VMEM((8, 2 * HD), F32),
+            pltpu.SemaphoreType.DMA((3, 2)),
+        ],
+        compiler_params=pltpu.CompilerParams(vmem_limit_bytes=64 * 2**20),
+    )(student, teacher, gap)
+    return student, teacher, gap.reshape(ROWS)
 
 
 def solution(mesh):

time: 67.1 us -> 66.1 us (0.985)
  local copies, waits for them, and re-layouts: 3.51 us -> 0 us
  Pallas kernels: 62.7 us -> 65.3 us
    unnamed x4 -> x0, local copies, waits for them, and re-layouts: 2.25 us -> none
    pallas_call x0 -> x1, Pallas kernels: none -> 2.22 us  [on_device(): pl.pallas_call(hand_over, out_shape=(jax.ShapeDtypeStruct(student.shape,...]
    slice x1 -> x0, local copies, waits for them, and re-layouts: 1.26 us -> none  [on_device(): return (student, teacher, gap[0, :ROWS])]
where the time goes in v3:
time: 66.1 us; the launch traced here: 65.9 us
  Pallas kernels  65.3 us (99%)
    pallas_call x1, Pallas kernels, on_device(): pl.pallas_call(kernel, out_shape=(jax.ShapeDtypeStruct((ROWS, HEADS_DEV *...  63.1 us
    pallas_call x1, Pallas kernels, on_device(): pl.pallas_call(hand_over, out_shape=(jax.ShapeDtypeStruct(student.shape,...  2.22 us

profile of v3, /device:TPU:1, one launch (start us, length us, event | category | flops | bytes accessed | tf_op | source)
XLA Modules:
  0.0 65.9 jit_solution(5828717494064521235)
XLA Ops:
  0.6 63.1 %shard_map.85 = (bf16[160,384]{1,0:T(8,128)(2,1)}, bf16[160,384]{1,0:T(8,128)(2,1)}, f32[8,256]{1,0:T(8,128)}) custom-call(bf16[160,384]{1,0:T(8,128)(2,1)} %q_ref.1, bf16[160,384]{1,0:T(8,128)(2,1)} %k_ref.1, bf16[160,384]{1,0:T(8,128)(2,1)} %v_ref.1, s32[64]{0:T(128)} %group_ref.1, s32[4,4]{1,0:T(4,128)} %mask_ref.1, f32[384]{0:T(512)} %gain_ref.1), custom_call_target="tpu_custom_call" | custom-call | tf_op jit(solution)/shard_map/pallas_call | solution.py:402
  63.7 2.2 %shard_map.86 = (bf16[160,384]{1,0:T(8,128)(2,1)}, bf16[160,384]{1,0:T(8,128)(2,1)}, f32[1,160]{1,0:T(1,128)}) custom-call(bf16[160,384]{1,0:T(8,128)(2,1)} %get-tuple-element.9.s_ref, bf16[160,384]{1,0:T(8,128)(2,1)} %get-tuple-element.10.t_ref, f32[8,256]{1,0:T(8,128)} %get-tuple-element.11.gap_ref), custom_call_target="tpu_custom_call" | custom-call | tf_op jit(solution)/shard_map/pallas_call | solution.py:441

commit v4 on v3

--- a/solution.py
+++ b/solution.py
@@ -63,9 +63,6 @@
         pltpu.make_async_copy(source, place, l_sem.at[HEADS_DEV, i])
         for i, (source, place) in enumerate(small)
     ]
-    for copy in own_copies + small_copies:
-        copy.start()
-
     barrier = pltpu.get_barrier_semaphore()
     nears = [k_device(1), k_device(-1)] + [q_device(shift) for shift in (1, -1, 2, -2)]
     for near in nears:
@@ -82,13 +79,16 @@
         return jnp.where(lax.rem(k, 2) == 1, lax.div(k + 1, 2), -lax.div(k, 2))
 
     legs = [(what, way, hop) for hop in (1, 2, 3) for what in (0, "q", 1, 2) for way in (1, -1)]
-    legs += [(0, 1, 4), (0, -1, 4), ("q", 1, 4), (1, 1, 4), (1, -1, 4), (2, 1, 4), (2, -1, 4)]
+    legs += [(what, way, 4) for what in (0, "q", 1, 2) for way in (1, -1)]
 
     def leg_copy(leg):
         what, way, hop = leg
         here, there = number(-way, hop - 1), number(-way, hop)
         if what == "q":
             ends = q_all.at[here], q_all.at[there]
+            if hop == 4:
+                heads = pl.ds(0, 1) if way == 1 else pl.ds(1, HEADS_DEV - 1)
+                ends = tuple(end.at[heads] for end in ends)
             near = q_device(way)
         else:
             ends = kv_all.at[what, here], kv_all.at[what, there]
@@ -134,15 +134,17 @@
                 if onward in legs:
                     leg_copy(onward).start()
 
-    def wait_last(what):
+    def wait_last(what, ways=(1, -1)):
         for leg in legs:
-            if leg[0] == what and leg[2] == 4:
+            if leg[0] == what and leg[1] in ways and leg[2] == 4:
                 leg_copy(leg).wait_recv()
 
     pl.semaphore_wait(barrier, len(nears) + PEERS - 1)
     for leg in legs:
         if leg[2] == 1:
             send_own(leg)
+    for copy in small_copies + own_copies:
+        copy.start()
 
     for copy in small_copies:
         copy.wait()
@@ -163,10 +165,10 @@
 
     lax.fori_loop(0, RING, set_bias, 0)
 
+    for hop in (1, 2, 3):
+        relay(hop)
     for copy in own_copies:
         copy.wait()
-    for hop in (1, 2, 3):
-        relay(hop)
     wait_last(0)
 
     def scores(h, k, score):
@@ -224,8 +226,8 @@
     def unpack(box, h, k, i):
         out = box[h, k, :ROWS, i * HD:(i + 1) * HD].astype(F32)
         stat = lax.dot_general(
-            box[h, k, ROWS:, :], spread[i], TN, preferred_element_type=F32
-        )[:ROWS]
+            box[h, k, ROWS:, :ROWS], spread[i], TN, preferred_element_type=F32
+        )
         return out, stat[:, :HD], stat[:, HD:]
 
     def merge(parts):
@@ -289,10 +291,10 @@
     joins += ((1, (3,), 7, (0, 1, 2)), (2, (4,), 8, (0, 1, 2)))
 
     def turn(g, carry):
-        for when, what in ((0, "q"), (1, 1), (2, 2)):
+        for when, what, ways in ((0, "q", (1,)), (1, "q", (-1,)), (1, 1, (1, -1)), (2, 2, (1, -1))):
             @pl.when(g == when)
-            def _(what=what):
-                wait_last(what)
+            def _(what=what, ways=ways):
+                wait_last(what, ways)
 
         for h, k in work(g):
             @pl.when(k >= 5)
@@ -398,7 +400,7 @@
 def on_device(queries, keys, values, block_group, group_mask, teacher_gain):
     vmem = pl.BlockSpec(memory_space=pltpu.VMEM)
     outside = pl.BlockSpec(memory_space=pltpu.HBM)
-    legs = 31
+    legs = 32
     student, teacher, gap = pl.pallas_call(
         kernel,
         out_shape=(

time: 66.1 us -> 65.6 us (level)
  no operation moved by 1% of the time
where the time goes in v4:
time: 65.6 us; the launch traced here: 65.4 us
  Pallas kernels  64.8 us (99%)
    pallas_call x1, Pallas kernels, on_device(): pl.pallas_call(kernel, out_shape=(jax.ShapeDtypeStruct((ROWS, HEADS_DEV *...  62.6 us
    pallas_call x1, Pallas kernels, on_device(): pl.pallas_call(hand_over, out_shape=(jax.ShapeDtypeStruct(student.shape,...  2.22 us

profile of v4, /device:TPU:1, one launch (start us, length us, event | category | flops | bytes accessed | tf_op | source)
XLA Modules:
  0.0 65.4 jit_solution(10694765965911155536)
XLA Ops:
  0.6 62.6 %shard_map.85 = (bf16[160,384]{1,0:T(8,128)(2,1)}, bf16[160,384]{1,0:T(8,128)(2,1)}, f32[8,256]{1,0:T(8,128)}) custom-call(bf16[160,384]{1,0:T(8,128)(2,1)} %q_ref.1, bf16[160,384]{1,0:T(8,128)(2,1)} %k_ref.1, bf16[160,384]{1,0:T(8,128)(2,1)} %v_ref.1, s32[64]{0:T(128)} %group_ref.1, s32[4,4]{1,0:T(4,128)} %mask_ref.1, f32[384]{0:T(512)} %gain_ref.1), custom_call_target="tpu_custom_call" | custom-call | tf_op jit(solution)/shard_map/pallas_call | solution.py:404
  63.2 2.2 %shard_map.86 = (bf16[160,384]{1,0:T(8,128)(2,1)}, bf16[160,384]{1,0:T(8,128)(2,1)}, f32[1,160]{1,0:T(1,128)}) custom-call(bf16[160,384]{1,0:T(8,128)(2,1)} %get-tuple-element.9.s_ref, bf16[160,384]{1,0:T(8,128)(2,1)} %get-tuple-element.10.t_ref, f32[8,256]{1,0:T(8,128)} %get-tuple-element.11.gap_ref), custom_call_target="tpu_custom_call" | custom-call | tf_op jit(solution)/shard_map/pallas_call | solution.py:443

commit v5 on v4

--- a/solution.py
+++ b/solution.py
@@ -274,16 +274,24 @@
         ])
         message(h, k, shift).start()
 
+    def send_far(h, k):
+        @pl.when(k >= 5)
+        def _():
+            across = jnp.where(h == 1, 2, -2)
+            message(h, k, jnp.where(k == 7, across, jnp.where(k == 5, 1, -1))).start()
+
     def work(g, last=False):
         h0, k0 = unit(2 * g)
         h1, k1 = unit(2 * g + 1)
         scores(h1, k1, score1)
         mix(h0, k0, score0)
         if not last:
+            send_far(h0, k0)
             h2, k2 = unit(2 * g + 2)
             scores(h2, k2, score0)
         mix(h1, k1, score1)
-        return (h0, k0), (h1, k1)
+        if not last:
+            send_far(h1, k1)
 
     scores(0, 5, score0)
 
@@ -296,11 +304,7 @@
             def _(what=what, ways=ways):
                 wait_last(what, ways)
 
-        for h, k in work(g):
-            @pl.when(k >= 5)
-            def _(h=h, k=k):
-                across = jnp.where(h == 1, 2, -2)
-                message(h, k, jnp.where(k == 7, across, jnp.where(k == 5, 1, -1))).start()
+        work(g)
 
         for k, others, first, heads in joins:
             mine = g == first + heads[0]

time: 65.6 us -> 66.9 us (1.020)
  Pallas kernels: 64.8 us -> 66.1 us
    pallas_call x1, Pallas kernels: 62.6 us -> 63.9 us  [on_device(): pl.pallas_call(kernel, out_shape=(jax.ShapeDtypeStruct((ROWS, HEADS_DEV *...]
where the time goes in v5:
time: 66.9 us; the launch traced here: 66.7 us
  Pallas kernels  66.1 us (99%)
    pallas_call x1, Pallas kernels, on_device(): pl.pallas_call(kernel, out_shape=(jax.ShapeDtypeStruct((ROWS, HEADS_DEV *...  63.9 us
    pallas_call x1, Pallas kernels, on_device(): pl.pallas_call(hand_over, out_shape=(jax.ShapeDtypeStruct(student.shape,...  2.22 us

profile of v5, /device:TPU:1, one launch (start us, length us, event | category | flops | bytes accessed | tf_op | source)
XLA Modules:
  0.0 66.7 jit_solution(12761869238066065005)
XLA Ops:
  0.6 63.9 %shard_map.85 = (bf16[160,384]{1,0:T(8,128)(2,1)}, bf16[160,384]{1,0:T(8,128)(2,1)}, f32[8,256]{1,0:T(8,128)}) custom-call(bf16[160,384]{1,0:T(8,128)(2,1)} %q_ref.1, bf16[160,384]{1,0:T(8,128)(2,1)} %k_ref.1, bf16[160,384]{1,0:T(8,128)(2,1)} %v_ref.1, s32[64]{0:T(128)} %group_ref.1, s32[4,4]{1,0:T(4,128)} %mask_ref.1, f32[384]{0:T(512)} %gain_ref.1), custom_call_target="tpu_custom_call" | custom-call | tf_op jit(solution)/shard_map/pallas_call | solution.py:408
  64.5 2.2 %shard_map.86 = (bf16[160,384]{1,0:T(8,128)(2,1)}, bf16[160,384]{1,0:T(8,128)(2,1)}, f32[1,160]{1,0:T(1,128)}) custom-call(bf16[160,384]{1,0:T(8,128)(2,1)} %get-tuple-element.9.s_ref, bf16[160,384]{1,0:T(8,128)(2,1)} %get-tuple-element.10.t_ref, f32[8,256]{1,0:T(8,128)} %get-tuple-element.11.gap_ref), custom_call_target="tpu_custom_call" | custom-call | tf_op jit(solution)/shard_map/pallas_call | solution.py:447
